TPU v7x, 32 devices: a whole 2x2x4 slice. The times are simulated.
32 devices in a mesh: src: 2 (over x), site: 16 (over z, y, core).
Axes of the slice: x: 2, y: 2, z: 4, core: 2. Of those that a mesh axis runs over, the one named last changes fastest.
Arguments:
- forward: bfloat16 [288, 65536], P(None, ('src', 'site')), parts along dimension 1, may hold values from -6 to 6
- seqprop: bfloat16 [512, 4608], P(('src', 'site')), parts along dimension 0, may hold values from -6 to 6
- sparse: int32 [4096], P(('src', 'site')), parts along dimension 0, may hold values from 0 to 2047, as said below
- owners: int32 [4096, 1], P(('src', 'site')), parts along dimension 0, may hold values from 0 to 15; in each aligned block of 128 rows (0 to 127, 128 to 255, ...) at most 16 rows name the same one
- contraction: int32 [1024, 6, 3], replicated, may hold values from 0 to 143
- momenta: int32 [64, 3], replicated, may hold values from -2 to 2
Outputs:
- corr: float32 [2048, 512], P(('src', 'site')), parts along dimension 0
There are 2 independent parts, one for each index of `src`. A program takes and returns all parts, laid end to end along the dimension named above; an argument that names none is the same for every part. Nothing has to cross between parts.
Inputs may be any that keep to these rules, and one draw needn't show every extreme that they name: `sparse`: each device's 128 entries are distinct local site numbers. `owners`: among the 128 blocks of one device at most 16 name one owner.
All inputs are finite; a program needn't handle non-finite values.
Results may differ from a plain program's by a relative error of at most 0.0035.
Values may be sent and summed in bfloat16 or wider, within the bound.
A program may use at most 64 MiB of HBM per device.

v0:
```python
import math

import jax
import jax.numpy as jnp
from jax import lax
from jax.sharding import PartitionSpec as P

LS = 64
TIMES = 4


def slot_ranks(owner_row, count):
    onehot = (owner_row[:, None] == jnp.arange(count, dtype=jnp.int32)[None, :]).astype(jnp.int32)
    before = jnp.cumsum(onehot, axis=0) - onehot
    return jnp.sum(before * onehot, axis=1)


def phase_moms(glob, momenta, sites_dev, nsite):
    device = glob // sites_dev
    per_time = nsite // TIMES
    spatial = device % per_time * sites_dev + glob % sites_dev
    coord_x = spatial % LS
    coord_y = spatial // LS % LS
    coord_z = spatial // (LS * LS) % LS
    dotted = (
        coord_x[:, None] * momenta[None, :, 0]
        + coord_y[:, None] * momenta[None, :, 1]
        + coord_z[:, None] * momenta[None, :, 2]
    )
    angle = (dotted % LS).astype(jnp.float32) * (2.0 * math.pi / LS)
    return (jnp.cos(angle).astype(jnp.bfloat16), (-jnp.sin(angle)).astype(jnp.bfloat16))


def contract(left, right, table):
    half = left.shape[0] // 2
    fre, fim, sre, sim = (left[:half], left[half:], right[:half], right[half:])
    acc_re = jnp.zeros((table.shape[0], left.shape[1]), jnp.float32)
    acc_im = jnp.zeros((table.shape[0], left.shape[1]), jnp.float32)
    for term in range(6):
        sign = 1.0 if term < 3 else -1.0
        ia, ib, ic = (table[:, term, 0], table[:, term, 1], table[:, term, 2])
        ar, ai = (fre[ia].astype(jnp.float32), fim[ia].astype(jnp.float32))
        br, bi = (fre[ib].astype(jnp.float32), fim[ib].astype(jnp.float32))
        cr, ci = (sre[ic].astype(jnp.float32), sim[ic].astype(jnp.float32))
        pr = ar * br - ai * bi
        pi = ar * bi + ai * br
        acc_re = acc_re + sign * (pr * cr - pi * ci)
        acc_im = acc_im + sign * (pr * ci + pi * cr)
    return (acc_re.astype(jnp.bfloat16), acc_im.astype(jnp.bfloat16))


def momentum_sums(bre, bim, wre, wim):
    first = jnp.dot(bre, wre, preferred_element_type=jnp.float32) - jnp.dot(
        bim, wim, preferred_element_type=jnp.float32
    )
    second = jnp.dot(bre, wim, preferred_element_type=jnp.float32) + jnp.dot(
        bim, wre, preferred_element_type=jnp.float32
    )
    return (first, second)


def to_columns(packed, comps):
    count = packed.shape[0]
    return jnp.transpose(packed.reshape(count, comps, -1), (1, 0, 2)).reshape(comps, -1)


def shards(forward, seqprop, sparse, owners, contraction, momenta):
    nsite = lax.axis_size("site")
    device = lax.axis_index("site")
    comps = forward.shape[0]
    sites_dev = forward.shape[1]
    nblocks = owners.shape[0]
    kept = sparse.shape[0]
    width = kept // nblocks
    slots = seqprop.shape[1] // (comps * width)
    owner_row = owners[:, 0]
    slot = slot_ranks(owner_row, nsite)
    fsel = jnp.take(forward, sparse, axis=1)
    glob = device * sites_dev + sparse
    pieces = jnp.transpose(fsel.reshape(comps, nblocks, width), (1, 0, 2))
    outgoing = (
        jnp.zeros((nsite, comps, slots, width), jnp.bfloat16).at[owner_row, :, slot, :].set(pieces)
    )
    numbers = (
        jnp.zeros((nsite, slots, width), jnp.int32)
        .at[owner_row, slot, :]
        .set(glob.reshape(nblocks, width))
    )
    arrived, arrived_sites = (
        lax.all_to_all(
            outgoing.reshape(nsite, -1), "site", split_axis=0, concat_axis=0, tiled=True
        ),
        lax.all_to_all(numbers.reshape(nsite, -1), "site", split_axis=0, concat_axis=0, tiled=True),
    )
    left = to_columns(arrived, comps)
    right = to_columns(seqprop, comps)
    wre, wim = phase_moms(arrived_sites.reshape(-1), momenta, sites_dev, nsite)
    span = left.shape[1] // TIMES
    bre, bim = contract(left, right, contraction)
    firsts = []
    seconds = []
    for tslice in range(TIMES):
        low = tslice * span
        first, second = momentum_sums(
            bre[:, low : low + span],
            bim[:, low : low + span],
            wre[low : low + span],
            wim[low : low + span],
        )
        firsts.append(first)
        seconds.append(second)
    total = lax.psum_scatter(
        jnp.concatenate(firsts + seconds, axis=1), "site", scatter_dimension=0, tiled=True
    )
    return total / jnp.sqrt(jnp.float32(kept * nsite / TIMES))


def solution(mesh):
    return jax.shard_map(
        shards,
        mesh=mesh,
        in_specs=(
            P(None, ("src", "site")),
            P(("src", "site"), None),
            P(("src", "site")),
            P(("src", "site"), None),
            P(),
            P(),
        ),
        out_specs=P(("src", "site"), None),
        check_vma=False,
    )
```

profile of v0, /device:TPU:0, one launch (start us, length us, event | category | flops | bytes accessed | tf_op | source)
XLA Modules:
  0.0 341.0 jit_solution(7123722769934674497)
XLA Ops:
  10.3 18.3 %scatter_fusion.1 = s32[16,16]{1,0:T(8,128)} fusion(s32[16,16]{1,0:T(8,128)} %broadcast.667, s32[128]{0:T(128)S(1)} %fusion.101, s32[128]{0:T(128)S(1)} %get-tuple-element.36), kind=kCustom, calls=%fused_computation.38 | custom fusion | bytes 2560 | tf_op jit(solution)/shard_map/scatter | solution.py:87
  28.6 7.4 %all-to-all-start.1 = ((s32[16,1,16]{2,1,0:T(1,128)}), s32[16,1,16]{2,1,0:T(1,128)S(1)}, u32[]{:S(2)}, u32[]{:S(2)}) async-start(s32[16,1,16]{2,1,0:T(1,128)} %bitcast.50), calls=%async_computation.1 | async-start | bytes 16384 | tf_op jit(solution)/shard_map/all_to_all | solution.py:93
  55.4 5.0 %gather_fusion.18 = bf16[1024,256]{1,0:T(8,128)(2,1)} fusion(bf16[144,256]{1,0:T(8,128)(2,1)S(1)} %copy.110, s32[1024]{0:T(1024)S(1)} %get-tuple-element.47), kind=kCustom, calls=%fused_computation.18 | custom fusion | bytes 1052672 | tf_op jit(solution)/shard_map/gather | solution.py:44
  79.1 5.0 %gather_fusion.35 = bf16[1024,256]{1,0:T(8,128)(2,1)} fusion(bf16[144,256]{1,0:T(8,128)(2,1)S(1)} %copy.108, s32[1024]{0:T(1024)S(1)} %get-tuple-element.38), kind=kCustom, calls=%fused_computation.35 | custom fusion | bytes 1052672 | tf_op jit(solution)/shard_map/gather | solution.py:44
  93.9 5.0 %gather_fusion.5 = bf16[1024,256]{1,0:T(8,128)(2,1)} fusion(bf16[144,256]{1,0:T(8,128)(2,1)S(1)} %copy.108, s32[1024]{0:T(1024)S(1)} %get-tuple-element.53), kind=kCustom, calls=%fused_computation.5 | custom fusion | bytes 1052672 | tf_op jit(solution)/shard_map/gather | solution.py:44
  98.9 7.6 %scatter_fusion = bf16[16,288,16]{1,2,0:T(8,128)(2,1)S(1)} fusion(bf16[16,288,16]{1,2,0:T(8,128)(2,1)S(1)} %broadcast.665, s32[128]{0:T(128)S(1)} %fusion.101, bf16[128,288]{1,0:T(8,128)(2,1)S(1)} %fusion.77), kind=kCustom, calls=%fused_computation.37 | custom fusion | bytes 222208 | tf_op jit(solution)/shard_map/scatter | solution.py:82
  112.2 6.0 %all-to-all-start = ((bf16[16,2,2304]{2,1,0:T(2,128)(2,1)}), bf16[16,2,2304]{2,1,0:T(2,128)(2,1)S(1)}, u32[]{:S(2)}, u32[]{:S(2)}) async-start(bf16[16,2,2304]{2,1,0:T(2,128)(2,1)} %reshape.1065), calls=%async_computation | async-start | bytes 294912 | tf_op jit(solution)/shard_map/all_to_all | solution.py:90
  120.4 6.0 %all-to-all-done = bf16[16,2,2304]{2,1,0:T(2,128)(2,1)S(1)} async-done(((bf16[16,2,2304]{2,1,0:T(2,128)(2,1)}), bf16[16,2,2304]{2,1,0:T(2,128)(2,1)S(1)}, u32[]{:S(2)}, u32[]{:S(2)}) %all-to-all-start) | async-done | bytes 147488 | tf_op jit(solution)/shard_map/all_to_all | solution.py:90
  133.9 5.0 %gather_fusion.13 = bf16[1024,256]{1,0:T(8,128)(2,1)} fusion(bf16[144,256]{1,0:T(8,128)(2,1)S(1)} %copy.102, s32[1024]{0:T(1024)S(1)} %get-tuple-element.49), kind=kCustom, calls=%fused_computation.13 | custom fusion | bytes 1052672 | tf_op jit(solution)/shard_map/gather | solution.py:42
  143.8 4.9 %gather_fusion.15 = bf16[1024,256]{1,0:T(8,128)(2,1)} fusion(bf16[144,256]{1,0:T(8,128)(2,1)S(1)} %copy.105, s32[1024]{0:T(1024)S(1)} %get-tuple-element.49), kind=kCustom, calls=%fused_computation.15 | custom fusion | bytes 1052672 | tf_op jit(solution)/shard_map/gather | solution.py:42
  148.7 5.0 %gather_fusion.16 = bf16[1024,256]{1,0:T(8,128)(2,1)} fusion(bf16[144,256]{1,0:T(8,128)(2,1)S(1)} %copy.105, s32[1024]{0:T(1024)S(1)} %get-tuple-element.48), kind=kCustom, calls=%fused_computation.16 | custom fusion | bytes 1052672 | tf_op jit(solution)/shard_map/gather | solution.py:43
  153.7 4.9 %gather_fusion.19 = bf16[1024,256]{1,0:T(8,128)(2,1)} fusion(bf16[144,256]{1,0:T(8,128)(2,1)S(1)} %copy.102, s32[1024]{0:T(1024)S(1)} %get-tuple-element.46), kind=kCustom, calls=%fused_computation.19 | custom fusion | bytes 1052672 | tf_op jit(solution)/shard_map/gather | solution.py:42
  158.7 5.0 %gather_fusion.21 = bf16[1024,256]{1,0:T(8,128)(2,1)} fusion(bf16[144,256]{1,0:T(8,128)(2,1)S(1)} %copy.105, s32[1024]{0:T(1024)S(1)} %get-tuple-element.46), kind=kCustom, calls=%fused_computation.21 | custom fusion | bytes 1052672 | tf_op jit(solution)/shard_map/gather | solution.py:42
  168.5 4.9 %gather_fusion.22 = bf16[1024,256]{1,0:T(8,128)(2,1)} fusion(bf16[144,256]{1,0:T(8,128)(2,1)S(1)} %copy.105, s32[1024]{0:T(1024)S(1)} %get-tuple-element.45), kind=kCustom, calls=%fused_computation.22 | custom fusion | bytes 1052672 | tf_op jit(solution)/shard_map/gather | solution.py:43
  183.4 4.9 %gather_fusion.26 = bf16[1024,256]{1,0:T(8,128)(2,1)} fusion(bf16[144,256]{1,0:T(8,128)(2,1)S(1)} %copy.102, s32[1024]{0:T(1024)S(1)} %get-tuple-element.42), kind=kCustom, calls=%fused_computation.26 | custom fusion | bytes 1052672 | tf_op jit(solution)/shard_map/gather | solution.py:43
  188.3 5.0 %gather_fusion.28 = bf16[1024,256]{1,0:T(8,128)(2,1)} fusion(bf16[144,256]{1,0:T(8,128)(2,1)S(1)} %copy.105, s32[1024]{0:T(1024)S(1)} %get-tuple-element.42), kind=kCustom, calls=%fused_computation.28 | custom fusion | bytes 1052672 | tf_op jit(solution)/shard_map/gather | solution.py:43
  193.3 5.0 %gather_fusion.1 = bf16[1024,256]{1,0:T(8,128)(2,1)} fusion(bf16[144,256]{1,0:T(8,128)(2,1)S(1)} %copy.102, s32[1024]{0:T(1024)S(1)} %get-tuple-element.55), kind=kCustom, calls=%fused_computation.1 | custom fusion | bytes 1052672 | tf_op jit(solution)/shard_map/gather | solution.py:42
  203.2 5.0 %gather_fusion.31 = bf16[1024,256]{1,0:T(8,128)(2,1)} fusion(bf16[144,256]{1,0:T(8,128)(2,1)S(1)} %copy.102, s32[1024]{0:T(1024)S(1)} %get-tuple-element.40), kind=kCustom, calls=%fused_computation.31 | custom fusion | bytes 1052672 | tf_op jit(solution)/shard_map/gather | solution.py:42
  208.1 5.0 %gather_fusion.33 = bf16[1024,256]{1,0:T(8,128)(2,1)} fusion(bf16[144,256]{1,0:T(8,128)(2,1)S(1)} %copy.105, s32[1024]{0:T(1024)S(1)} %get-tuple-element.40), kind=kCustom, calls=%fused_computation.33 | custom fusion | bytes 1052672 | tf_op jit(solution)/shard_map/gather | solution.py:42
  227.9 4.9 %gather_fusion.4 = bf16[1024,256]{1,0:T(8,128)(2,1)} fusion(bf16[144,256]{1,0:T(8,128)(2,1)S(1)} %copy.105, s32[1024]{0:T(1024)S(1)} %get-tuple-element.54), kind=kCustom, calls=%fused_computation.4 | custom fusion | bytes 1052672 | tf_op jit(solution)/shard_map/gather | solution.py:43
  232.8 4.9 %gather_fusion.10 = bf16[1024,256]{1,0:T(8,128)(2,1)} fusion(bf16[144,256]{1,0:T(8,128)(2,1)S(1)} %copy.105, s32[1024]{0:T(1024)S(1)} %get-tuple-element.51), kind=kCustom, calls=%fused_computation.10 | custom fusion | bytes 1052672 | tf_op jit(solution)/shard_map/gather | solution.py:43
  242.7 4.9 %gather_fusion.7 = bf16[1024,256]{1,0:T(8,128)(2,1)} fusion(bf16[144,256]{1,0:T(8,128)(2,1)S(1)} %copy.102, s32[1024]{0:T(1024)S(1)} %get-tuple-element.52), kind=kCustom, calls=%fused_computation.7 | custom fusion | bytes 1052672 | tf_op jit(solution)/shard_map/gather | solution.py:42
  252.9 7.7 %fusion.23 = bf16[1024,256]{1,0:T(8,128)(2,1)S(1)} fusion(bf16[1024,256]{1,0:T(8,128)(2,1)} %gather_fusion.5, bf16[1024,256]{1,0:T(8,128)(2,1)} %gather_fusion.6, bf16[1024,256]{1,0:T(8,128)(2,1)S(1)} %gather_fusion.11, bf16[1024,256]{1,0:T(8,128)(2,1)S(1)} %gather_fusion.12, bf16[1024,256]{1,0:T(8,128)(2,1)S(1)} %gather_fusion.17, ...), kind=kLoop, calls=%fused_computation.118 | loop fusion | flops 25952256 | bytes 19398656 | tf_op jit(solution)/shard_map/convert_element_type | solution.py:49
  272.8 59.8 %reduce-scatter.4.cloned.1.call-done = f32[64,512]{1,0:T(8,128)} async-done(((f32[1024,512]{1,0:T(8,128)}), f32[64,512]{1,0:T(8,128)}) %reduce-scatter.4.cloned.1.call-update) | async-done | bytes 131088 | tf_op jit(solution)/shard_map/reduce_scatter | solution.py:112
  (159 shorter events, 129.9 us)
Async XLA Ops:
  6.5 31.2 %copy-start.32 = (bf16[288,2048]{1,0:T(8,128)(2,1)S(1)}, bf16[288,2048]{1,0:T(8,128)(2,1)}, u32[]{:S(2)}) copy-start(bf16[288,2048]{1,0:T(8,128)(2,1)} %param.6) | copy-start | bytes 3538948
  7.4 31.3 %copy-start.33 = (bf16[16,4608]{1,0:T(8,128)(2,1)S(1)}, bf16[16,4608]{1,0:T(8,128)(2,1)}, u32[]{:S(2)}) copy-start(bf16[16,4608]{1,0:T(8,128)(2,1)} %param.7) | copy-start | bytes 442372
  28.6 83.6 %all-to-all-start.1 = ((s32[16,1,16]{2,1,0:T(1,128)}), s32[16,1,16]{2,1,0:T(1,128)S(1)}, u32[]{:S(2)}, u32[]{:S(2)}) async-start(s32[16,1,16]{2,1,0:T(1,128)} %bitcast.50), calls=%async_computation.1 | async-start | bytes 16384 | tf_op jit(solution)/shard_map/all_to_all | solution.py:93
  112.2 14.2 %all-to-all-start = ((bf16[16,2,2304]{2,1,0:T(2,128)(2,1)}), bf16[16,2,2304]{2,1,0:T(2,128)(2,1)S(1)}, u32[]{:S(2)}, u32[]{:S(2)}) async-start(bf16[16,2,2304]{2,1,0:T(2,128)(2,1)} %reshape.1065), calls=%async_computation | async-start | bytes 294912 | tf_op jit(solution)/shard_map/all_to_all | solution.py:90
  118.2 214.4 %reduce-scatter.4.cloned.1.call-start = ((), (), s32[]{:S(2)}) async-start(), calls=%async_computation.3 | async-start | bytes 2228224 | tf_op jit(solution)/shard_map/reduce_scatter | solution.py:112
  252.6 8.0 %copy-start.3 = (bf16[1024,256]{1,0:T(8,128)(2,1)S(1)}, bf16[1024,256]{1,0:T(8,128)(2,1)}, u32[]{:S(2)}) copy-start(bf16[1024,256]{1,0:T(8,128)(2,1)} %gather_fusion.30) | copy-start | bytes 1572868
  252.6 8.0 %copy-start.4 = (bf16[1024,256]{1,0:T(8,128)(2,1)S(1)}, bf16[1024,256]{1,0:T(8,128)(2,1)}, u32[]{:S(2)}) copy-start(bf16[1024,256]{1,0:T(8,128)(2,1)} %gather_fusion.35) | copy-start | bytes 1572868
  252.6 8.0 %copy-start.5 = (bf16[1024,256]{1,0:T(8,128)(2,1)S(1)}, bf16[1024,256]{1,0:T(8,128)(2,1)}, u32[]{:S(2)}) copy-start(bf16[1024,256]{1,0:T(8,128)(2,1)} %gather_fusion.36) | copy-start | bytes 1572868
  252.6 8.0 %copy-start.6 = (bf16[1024,256]{1,0:T(8,128)(2,1)S(1)}, bf16[1024,256]{1,0:T(8,128)(2,1)}, u32[]{:S(2)}) copy-start(bf16[1024,256]{1,0:T(8,128)(2,1)} %gather_fusion.6) | copy-start | bytes 1572868
  252.6 8.0 %copy-start.7 = (bf16[1024,256]{1,0:T(8,128)(2,1)S(1)}, bf16[1024,256]{1,0:T(8,128)(2,1)}, u32[]{:S(2)}) copy-start(bf16[1024,256]{1,0:T(8,128)(2,1)} %gather_fusion.5) | copy-start | bytes 1572868
  252.7 8.0 %copy-start.8 = (bf16[1024,256]{1,0:T(8,128)(2,1)S(1)}, bf16[1024,256]{1,0:T(8,128)(2,1)}, u32[]{:S(2)}) copy-start(bf16[1024,256]{1,0:T(8,128)(2,1)} %gather_fusion.13) | copy-start | bytes 1572868
  252.8 8.1 %copy-start.19 = (bf16[1024,256]{1,0:T(8,128)(2,1)S(1)}, bf16[1024,256]{1,0:T(8,128)(2,1)}, u32[]{:S(2)}) copy-start(bf16[1024,256]{1,0:T(8,128)(2,1)} %gather_fusion.28) | copy-start | bytes 1572868
  252.8 8.2 %copy-start.20 = (bf16[1024,256]{1,0:T(8,128)(2,1)S(1)}, bf16[1024,256]{1,0:T(8,128)(2,1)}, u32[]{:S(2)}) copy-start(bf16[1024,256]{1,0:T(8,128)(2,1)} %gather_fusion.1) | copy-start | bytes 1572868
  252.8 8.4 %copy-start.21 = (bf16[1024,256]{1,0:T(8,128)(2,1)S(1)}, bf16[1024,256]{1,0:T(8,128)(2,1)}, u32[]{:S(2)}) copy-start(bf16[1024,256]{1,0:T(8,128)(2,1)} %gather_fusion.3) | copy-start | bytes 1572868
  252.8 8.5 %copy-start.22 = (bf16[1024,256]{1,0:T(8,128)(2,1)S(1)}, bf16[1024,256]{1,0:T(8,128)(2,1)}, u32[]{:S(2)}) copy-start(bf16[1024,256]{1,0:T(8,128)(2,1)} %gather_fusion.31) | copy-start | bytes 1572868
  252.8 8.7 %copy-start.23 = (bf16[1024,256]{1,0:T(8,128)(2,1)S(1)}, bf16[1024,256]{1,0:T(8,128)(2,1)}, u32[]{:S(2)}) copy-start(bf16[1024,256]{1,0:T(8,128)(2,1)} %gather_fusion.33) | copy-start | bytes 1572868
  252.8 8.8 %copy-start.24 = (bf16[1024,256]{1,0:T(8,128)(2,1)S(1)}, bf16[1024,256]{1,0:T(8,128)(2,1)}, u32[]{:S(2)}) copy-start(bf16[1024,256]{1,0:T(8,128)(2,1)} %gather_fusion.32) | copy-start | bytes 1572868
  252.8 8.9 %copy-start.25 = (bf16[1024,256]{1,0:T(8,128)(2,1)S(1)}, bf16[1024,256]{1,0:T(8,128)(2,1)}, u32[]{:S(2)}) copy-start(bf16[1024,256]{1,0:T(8,128)(2,1)} %gather_fusion.34) | copy-start | bytes 1572868
  252.8 9.1 %copy-start.26 = (bf16[1024,256]{1,0:T(8,128)(2,1)S(1)}, bf16[1024,256]{1,0:T(8,128)(2,1)}, u32[]{:S(2)}) copy-start(bf16[1024,256]{1,0:T(8,128)(2,1)} %gather_fusion.2) | copy-start | bytes 1572868
  252.8 9.2 %copy-start.27 = (bf16[1024,256]{1,0:T(8,128)(2,1)S(1)}, bf16[1024,256]{1,0:T(8,128)(2,1)}, u32[]{:S(2)}) copy-start(bf16[1024,256]{1,0:T(8,128)(2,1)} %gather_fusion.4) | copy-start | bytes 1572868
  252.9 9.4 %copy-start.28 = (bf16[1024,256]{1,0:T(8,128)(2,1)S(1)}, bf16[1024,256]{1,0:T(8,128)(2,1)}, u32[]{:S(2)}) copy-start(bf16[1024,256]{1,0:T(8,128)(2,1)} %gather_fusion.10) | copy-start | bytes 1572868
  252.9 9.5 %copy-start.29 = (bf16[1024,256]{1,0:T(8,128)(2,1)S(1)}, bf16[1024,256]{1,0:T(8,128)(2,1)}, u32[]{:S(2)}) copy-start(bf16[1024,256]{1,0:T(8,128)(2,1)} %gather_fusion.8) | copy-start | bytes 1572868
  252.9 9.6 %copy-start.30 = (bf16[1024,256]{1,0:T(8,128)(2,1)S(1)}, bf16[1024,256]{1,0:T(8,128)(2,1)}, u32[]{:S(2)}) copy-start(bf16[1024,256]{1,0:T(8,128)(2,1)} %gather_fusion.7) | copy-start | bytes 1572868
  252.9 9.8 %copy-start.31 = (bf16[1024,256]{1,0:T(8,128)(2,1)S(1)}, bf16[1024,256]{1,0:T(8,128)(2,1)}, u32[]{:S(2)}) copy-start(bf16[1024,256]{1,0:T(8,128)(2,1)} %gather_fusion.9) | copy-start | bytes 1572868
  (14 other events, 100.7 us)
Sparse Core Ops, SparseCore 0:
  272.9 59.5 reduce-scatter.3
where the time goes:
time: 342 us; the launch traced here: 341 us
  local copies, waits for them, and re-layouts  220 us (64%)
  waiting for transfers between devices  65.8 us (19%)
  other arithmetic  23.3 us (7%)
  between operations  14.2 us (4%)
  starting transfers between devices  13.6 us (4%)
  matrix products  4.48 us (1%)
    reduce_scatter x1, waiting for transfers between devices, shards(): lax.psum_scatter(jnp.concatenate(firsts + seconds, axis=1), 'site', scatt...  59.8 us
    gather x12, local copies, waits for them, and re-layouts, contract(): ar, ai = (fre[ia].astype(jnp.float32), fim[ia].astype(jnp.float32))  59.4 us
    gather x12, local copies, waits for them, and re-layouts, contract(): br, bi = (fre[ib].astype(jnp.float32), fim[ib].astype(jnp.float32))  59.3 us
    gather x12, local copies, waits for them, and re-layouts, contract(): cr, ci = (sre[ic].astype(jnp.float32), sim[ic].astype(jnp.float32))  55.3 us
    scatter x1, local copies, waits for them, and re-layouts, shards(): numbers = jnp.zeros((nsite, slots, width), jnp.int32).at[owner_row, slot,...  18.3 us
    convert_element_type x2, other arithmetic, contract(): return (acc_re.astype(jnp.bfloat16), acc_im.astype(jnp.bfloat16))  11.4 us
    scatter x2, local copies, waits for them, and re-layouts, shards(): jnp.zeros((nsite, comps, slots, width), jnp.bfloat16)  8.16 us
    all_to_all x1, starting transfers between devices, shards(): lax.all_to_all(numbers.reshape(nsite, -1), 'site', split_axis=0, concat_a...  7.41 us
  transfers between devices with their start and end apart: 3, of which 2 were waited for; matrix products, arithmetic and copies ran while one was open for 22% of the time, Pallas kernels for 0%

commit v1 on v0

v1 whole, which is shorter than its diff:
```python
import functools
import math

import jax
import jax.numpy as jnp
from jax import lax
from jax.experimental import pallas as pl
from jax.experimental.pallas import tpu as pltpu
from jax.sharding import PartitionSpec as P

LS = 64
TIMES = 4
TERMS = 6
LANES = 128
DEPTH = 256
ROWS = 128
F32 = jnp.float32
BF16 = jnp.bfloat16
I32 = jnp.int32


def iota(shape, dim):
    return lax.broadcasted_iota(I32, shape, dim)


def onehot(mask):
    return jnp.where(mask, 1.0, 0.0).astype(BF16)


def column(row):
    n = row.shape[1]
    return jnp.broadcast_to(row.astype(F32), (n, n)).T.astype(I32)


def kernel(
    nsite,
    fwd_ref,
    seq_ref,
    sparse_ref,
    owner_ref,
    table_ref,
    mom_ref,
    out_ref,
    msg32,
    msgs,
    got,
    tabs,
    tabt,
    tf,
    ts,
    phase,
    ohf,
    ohs,
    gat,
    prod,
    parts,
    acc,
    send1,
    recv1,
    send2,
    recv2,
):
    me = lax.axis_index("site")
    comps, sites_dev = fwd_ref.shape
    half = comps // 2
    sel = sparse_ref.shape[1]
    slots = seq_ref.shape[1] // comps
    kall = table_ref.shape[2]
    kdev = kall // nsite
    moms = mom_ref.shape[1]
    per_time = nsite // TIMES
    pitch = msgs.shape[1]

    barrier = pltpu.get_barrier_semaphore()

    def greet(step, _):
        dst = lax.rem(me + step, nsite)
        pl.semaphore_signal(
            barrier, inc=1, device_id={"site": dst}, device_id_type=pl.DeviceIdType.MESH
        )
        return 0

    lax.fori_loop(1, nsite, greet, 0)

    flat = seq_ref.shape[1]
    for c in range(pitch):
        low = c * LANES
        if low >= flat:
            piece = jnp.zeros((nsite, LANES), F32)
        else:
            width = min(LANES, flat - low)
            piece = seq_ref[:, low : low + width].astype(F32)
            if width < LANES:
                piece = jnp.concatenate([piece, jnp.zeros((nsite, LANES - width), F32)], axis=1)
        msg32[pl.ds(c, nsite, stride=pitch), :] = piece
    msgs[...] = msg32[...].reshape(nsite, pitch, LANES).astype(BF16)

    pl.semaphore_wait(barrier, nsite - 1)

    def seq_copy(slot, peer):
        return pltpu.make_async_remote_copy(
            src_ref=msgs.at[peer],
            dst_ref=got.at[slot],
            send_sem=send1.at[peer],
            recv_sem=recv1.at[slot],
            device_id={"site": peer},
            device_id_type=pl.DeviceIdType.MESH,
        )

    def send_seq(step, _):
        dst = lax.rem(me + step, nsite)
        seq_copy(me, dst).start()
        return 0

    lax.fori_loop(1, nsite, send_seq, 0)
    got[me] = msgs[me]

    sparse = sparse_ref[...]
    pick = onehot(iota((sites_dev, sel), 0) == sparse)
    fsel = jnp.dot(fwd_ref[...], pick, preferred_element_type=F32).astype(BF16)
    tf[...] = jnp.zeros_like(tf)
    tf[0:half, 0:sel] = fsel[:half]
    tf[0:half, sel:] = fsel[half:]

    tabs[...] = jnp.zeros_like(tabs)
    for m in range(TERMS):
        tabs[3 * m : 3 * m + 3, :] = table_ref[m].astype(F32)
    for c in range(kall // LANES):
        tabt[c * LANES : (c + 1) * LANES, :] = tabs[:, c * LANES : (c + 1) * LANES].T.astype(I32)

    def forward_part(ci, _):
        base = pl.multiple_of(ci * ROWS, ROWS)
        idx = tabt[pl.ds(base, ROWS), :]
        lane = iota((ROWS, DEPTH), 1)
        for m in range(TERMS):
            for f in range(2):
                low = (2 * m + f) * ROWS
                ohf[low : low + ROWS, :] = onehot(idx[:, 3 * m + f : 3 * m + f + 1] == lane)
            low = m * ROWS
            ohs[ci, low : low + ROWS, :] = onehot(idx[:, 3 * m + 2 : 3 * m + 3] == lane)
        gat[...] = jnp.dot(ohf[...], tf[...], preferred_element_type=F32)
        for m in range(TERMS):
            la, lb, low = 2 * m * ROWS, (2 * m + 1) * ROWS, m * ROWS
            ar, ai = gat[la : la + ROWS, :sel], gat[la : la + ROWS, sel:]
            br, bi = gat[lb : lb + ROWS, :sel], gat[lb : lb + ROWS, sel:]
            prod[ci, low : low + ROWS, :sel] = ar * br - ai * bi
            prod[ci, low : low + ROWS, sel:] = ar * bi + ai * br
        return 0

    lax.fori_loop(0, kall // ROWS, forward_part, 0)

    spatial = lax.rem(me, per_time) * sites_dev + column(sparse)
    xs, ys, zs = spatial & (LS - 1), (spatial >> 6) & (LS - 1), (spatial >> 12) & (LS - 1)
    mom = mom_ref[...]
    mom = jnp.concatenate([mom, mom], axis=1)
    dotted = xs * mom[0:1] + ys * mom[1:2] + zs * mom[2:3]
    second = iota((sel, 2 * moms), 1) >= moms
    quarter = LS // 4
    for part in range(2):
        shift = jnp.where(second, quarter, 0) - quarter * part
        angle = ((dotted + shift) & (LS - 1)).astype(F32) * (2.0 * math.pi / LS)
        phase[part * sel : (part + 1) * sel, :] = jnp.cos(angle).astype(BF16)

    owner = owner_ref[...]
    earlier = (column(owner) == owner) & (iota((sel, sel), 0) < iota((sel, sel), 1))
    rank = jnp.sum(jnp.where(earlier, 1.0, 0.0), axis=0, keepdims=True).astype(I32)
    key = owner * slots + rank

    def wait_seq(step, _):
        src = lax.rem(me + nsite - step, nsite)
        seq_copy(src, src).wait_recv()
        return 0

    lax.fori_loop(1, nsite, wait_seq, 0)

    per_row = LANES // slots

    def select(o, total):
        rows = got[o].astype(F32)
        pieces = []
        group = iota((8, LANES), 1) // slots
        for g in range(comps // 8):
            row = g * 8 // per_row
            want = g * 8 % per_row + iota((8, LANES), 0)
            line = jnp.broadcast_to(rows[row : row + 1, :], (8, LANES))
            pieces.append(jnp.where(group == want, line, 0.0))
        spread = jnp.concatenate(pieces, axis=0).astype(BF16)
        match = onehot(o * slots + iota((LANES, sel), 0) % slots == key)
        return total + jnp.dot(spread, match, preferred_element_type=F32)

    ssel = lax.fori_loop(0, nsite, select, jnp.zeros((comps, sel), F32)).astype(BF16)
    ts[...] = jnp.zeros_like(ts)
    ts[0:half, 0:sel] = ssel[:half]
    ts[0:half, sel:] = ssel[half:]

    def part_copy(slot, peer):
        return pltpu.make_async_remote_copy(
            src_ref=parts.at[peer],
            dst_ref=acc.at[slot],
            send_sem=send2.at[peer],
            recv_sem=recv2.at[slot],
            device_id={"site": peer},
            device_id_type=pl.DeviceIdType.MESH,
        )

    kpad = parts.shape[1]
    nchunks = kall // ROWS
    mine = me * kdev // ROWS

    def finish(step, _):
        ci = lax.rem(mine + 1 + step, nchunks)
        gs = jnp.dot(ohs[ci], ts[...], preferred_element_type=F32)
        re = jnp.zeros((ROWS, sel), F32)
        im = jnp.zeros((ROWS, sel), F32)
        for m in range(TERMS):
            low = m * ROWS
            cr, cim = gs[low : low + ROWS, :sel], gs[low : low + ROWS, sel:]
            pr, pim = prod[ci, low : low + ROWS, :sel], prod[ci, low : low + ROWS, sel:]
            tr, tim = pr * cr - pim * cim, pr * cim + pim * cr
            if m < 3:
                re, im = re + tr, im + tim
            else:
                re, im = re - tr, im - tim
        block = jnp.concatenate([re, im], axis=1).astype(BF16)
        sums = jnp.dot(block, phase[...], preferred_element_type=F32)
        for h in range(ROWS // kdev):
            piece = sums[h * kdev : (h + 1) * kdev]
            if kpad > kdev:
                piece = jnp.concatenate([piece, jnp.zeros((kpad - kdev, LANES), F32)], axis=0)
            dst = ci * (ROWS // kdev) + h
            parts[dst] = piece.astype(BF16)

            @pl.when(dst != me)
            def _():
                part_copy(me, dst).start()

        return 0

    lax.fori_loop(0, nchunks, finish, 0)
    acc[me] = parts[me]

    def wait_part(step, _):
        src = lax.rem(me + nsite - step, nsite)
        part_copy(src, src).wait_recv()
        return 0

    lax.fori_loop(1, nsite, wait_part, 0)

    scale = 1.0 / math.sqrt(sel * nsite / TIMES)
    firsts, seconds = [], []
    for t in range(TIMES):
        total = jnp.zeros((kpad, LANES), F32)
        for g in range(per_time):
            total = total + acc[t * per_time + g].astype(F32)
        total = total[:kdev] * scale
        firsts.append(total[:, :moms])
        seconds.append(total[:, moms:])
    out_ref[...] = jnp.concatenate(firsts + seconds, axis=1)

    def drain(step, _):
        dst = lax.rem(me + step, nsite)
        seq_copy(me, dst).wait_send()
        part_copy(me, dst).wait_send()
        return 0

    lax.fori_loop(1, nsite, drain, 0)


def shards(forward, seqprop, sparse, owners, contraction, momenta):
    nsite = lax.axis_size("site")
    comps = forward.shape[0]
    kept = sparse.shape[0]
    kall = contraction.shape[0]
    moms = momenta.shape[0]
    flat = seqprop.shape[1]
    pitch = -(-flat // (16 * LANES)) * 16
    kdev = kall // nsite
    kpad = max(16, kdev)
    nchunks = kall // ROWS
    vmem = pl.BlockSpec(memory_space=pltpu.VMEM)
    return pl.pallas_call(
        functools.partial(kernel, nsite),
        out_shape=jax.ShapeDtypeStruct((kdev, 2 * TIMES * moms), F32),
        in_specs=[vmem] * 6,
        out_specs=vmem,
        scratch_shapes=[
            pltpu.VMEM((nsite * pitch, LANES), F32),
            pltpu.VMEM((nsite, pitch, LANES), BF16),
            pltpu.VMEM((nsite, pitch, LANES), BF16),
            pltpu.VMEM((LANES, kall), F32),
            pltpu.VMEM((kall, LANES), I32),
            pltpu.VMEM((DEPTH, 2 * kept), BF16),
            pltpu.VMEM((DEPTH, 2 * kept), BF16),
            pltpu.VMEM((2 * kept, 2 * moms), BF16),
            pltpu.VMEM((2 * TERMS * ROWS, DEPTH), BF16),
            pltpu.VMEM((nchunks, TERMS * ROWS, DEPTH), BF16),
            pltpu.VMEM((2 * TERMS * ROWS, 2 * kept), F32),
            pltpu.VMEM((nchunks, TERMS * ROWS, 2 * kept), F32),
            pltpu.VMEM((nsite, kpad, LANES), BF16),
            pltpu.VMEM((nsite, kpad, LANES), BF16),
            pltpu.SemaphoreType.DMA((nsite,)),
            pltpu.SemaphoreType.DMA((nsite,)),
            pltpu.SemaphoreType.DMA((nsite,)),
            pltpu.SemaphoreType.DMA((nsite,)),
        ],
        compiler_params=pltpu.CompilerParams(
            collective_id=0, has_side_effects=True, vmem_limit_bytes=48 * 1024 * 1024
        ),
    )(
        forward,
        seqprop,
        sparse.reshape(1, kept),
        owners.T,
        jnp.transpose(contraction, (1, 2, 0)),
        momenta.T,
    )


def solution(mesh):
    return jax.shard_map(
        shards,
        mesh=mesh,
        in_specs=(
            P(None, ("src", "site")),
            P(("src", "site"), None),
            P(("src", "site")),
            P(("src", "site"), None),
            P(),
            P(),
        ),
        out_specs=P(("src", "site"), None),
        check_vma=False,
    )
```

time: 342 us -> 28.1 us (0.08)
  the two profiles are of different devices: /device:TPU:0 before, /device:TPU:1 now
where the time goes in v1:
time: 28.1 us; the launch traced here: 27.8 us
  Pallas kernels  22.1 us (79%)
  local copies, waits for them, and re-layouts  5.72 us (20%)
    pallas_call x1, Pallas kernels, shards(): pl.pallas_call(functools.partial(kernel, nsite), out_shape=jax.ShapeDtype...  22.1 us
    unnamed x13, local copies, waits for them, and re-layouts  5.72 us

profile of v1, /device:TPU:1, one launch (start us, length us, event | category | flops | bytes accessed | tf_op | source)
XLA Modules:
  0.0 27.8 jit_solution(16915793667907321555)
XLA Ops:
  0.0 0.0 copy-start
  0.0 1.3 %copy-done = bf16[288,2048]{1,0:T(8,128)(2,1)S(1)} copy-done((bf16[288,2048]{1,0:T(8,128)(2,1)S(1)}, bf16[288,2048]{1,0:T(8,128)(2,1)}, u32[]{:S(2)}) %copy-start) | copy-done | bytes 1179672
  1.3 0.0 copy-start.1
  1.3 0.9 %copy-done.1 = bf16[16,4608]{1,0:T(8,128)(2,1)S(1)} copy-done((bf16[16,4608]{1,0:T(8,128)(2,1)S(1)}, bf16[16,4608]{1,0:T(8,128)(2,1)}, u32[]{:S(2)}) %copy-start.1) | copy-done | bytes 147480
  2.2 0.0 copy-start.2
  2.2 0.9 %copy-done.2 = s32[1024,6,3]{0,2,1:T(4,128)S(1)} copy-done((s32[1024,6,3]{0,2,1:T(4,128)S(1)}, s32[1024,6,3]{0,2,1:T(4,128)}, u32[]{:S(2)}) %copy-start.2) | copy-done | bytes 73752
  3.1 0.0 copy-start.3
  3.1 0.7 %copy-done.3 = s32[64,3]{0,1:T(4,128)S(1)} copy-done((s32[64,3]{0,1:T(4,128)S(1)}, s32[64,3]{0,1:T(4,128)}, u32[]{:S(2)}) %copy-start.3) | copy-done | bytes 792
  3.8 0.0 copy-start.4
  3.8 0.7 %copy-done.4 = s32[128]{0:T(128)S(1)} copy-done((s32[128]{0:T(128)S(1)}, s32[128]{0:T(128)}, u32[]{:S(2)}) %copy-start.4) | copy-done | bytes 536
  4.4 0.0 copy-start.5
  4.4 0.7 %copy-done.5 = s32[128,1]{0,1:T(1,128)S(1)} copy-done((s32[128,1]{0,1:T(1,128)S(1)}, s32[128,1]{0,1:T(1,128)}, u32[]{:S(2)}) %copy-start.5) | copy-done | bytes 536
  5.1 22.1 %shard_map.64 = f32[64,512]{1,0:T(8,128)S(1)} custom-call(bf16[288,2048]{1,0:T(8,128)(2,1)S(1)} %copy-done, bf16[16,4608]{1,0:T(8,128)(2,1)S(1)} %copy-done.1, s32[1,128]{1,0:T(1,128)S(1)} %bitcast.6, s32[1,128]{1,0:T(1,128)S(1)} %bitcast.7, s32[6,3,1024]{2,1,0:T(4,128)S(1)} %bitcast.4, s32[3,64]{1,0:T(4,128)S(1)} %bitcast.5), custom_call_target="tpu_custom_call" | custom-call | tf_op jit(solution)/shard_map/pallas_call | solution.py:281
  27.2 0.7 %copy.8 = f32[64,512]{1,0:T(8,128)} copy(f32[64,512]{1,0:T(8,128)S(1)} %shard_map.64) | data formatting | bytes 262144
Async XLA Ops:
  0.0 1.3 %copy-start = (bf16[288,2048]{1,0:T(8,128)(2,1)S(1)}, bf16[288,2048]{1,0:T(8,128)(2,1)}, u32[]{:S(2)}) copy-start(bf16[288,2048]{1,0:T(8,128)(2,1)} %fwd_ref.1) | copy-start | bytes 3538948
  1.3 0.9 %copy-start.1 = (bf16[16,4608]{1,0:T(8,128)(2,1)S(1)}, bf16[16,4608]{1,0:T(8,128)(2,1)}, u32[]{:S(2)}) copy-start(bf16[16,4608]{1,0:T(8,128)(2,1)} %seq_ref.1) | copy-start | bytes 442372
  2.2 0.9 %copy-start.2 = (s32[1024,6,3]{0,2,1:T(4,128)S(1)}, s32[1024,6,3]{0,2,1:T(4,128)}, u32[]{:S(2)}) copy-start(s32[1024,6,3]{0,2,1:T(4,128)} %param.10) | copy-start | bytes 221188
  3.1 0.7 %copy-start.3 = (s32[64,3]{0,1:T(4,128)S(1)}, s32[64,3]{0,1:T(4,128)}, u32[]{:S(2)}) copy-start(s32[64,3]{0,1:T(4,128)} %param.11) | copy-start | bytes 2308
  3.8 0.7 %copy-start.4 = (s32[128]{0:T(128)S(1)}, s32[128]{0:T(128)}, u32[]{:S(2)}) copy-start(s32[128]{0:T(128)} %param.8) | copy-start | bytes 1540
  4.4 0.7 %copy-start.5 = (s32[128,1]{0,1:T(1,128)S(1)}, s32[128,1]{0,1:T(1,128)}, u32[]{:S(2)}) copy-start(s32[128,1]{0,1:T(1,128)} %param.9) | copy-start | bytes 1540

commit v2 on v1

--- a/solution.py
+++ b/solution.py
@@ -14,6 +14,8 @@
 LANES = 128
 DEPTH = 256
 ROWS = 128
+LAG = 3
+EARLY = 2
 F32 = jnp.float32
 BF16 = jnp.bfloat16
 I32 = jnp.int32
@@ -34,13 +36,20 @@
 
 def kernel(
     nsite,
+    fwd_hbm,
+    seq_hbm,
+    sparse_hbm,
+    owner_hbm,
+    table_hbm,
+    mom_hbm,
+    out_ref,
     fwd_ref,
     seq_ref,
     sparse_ref,
     owner_ref,
     table_ref,
     mom_ref,
-    out_ref,
+    load_sem,
     msg32,
     msgs,
     got,
@@ -53,12 +62,16 @@
     ohs,
     gat,
     prod,
+    halves,
+    others,
     parts,
     acc,
     send1,
     recv1,
     send2,
     recv2,
+    send3,
+    recv3,
 ):
     me = lax.axis_index("site")
     comps, sites_dev = fwd_ref.shape
@@ -71,6 +84,22 @@
     per_time = nsite // TIMES
     pitch = msgs.shape[1]
 
+    loads = [
+        pltpu.make_async_copy(source, target, load_sem.at[n])
+        for n, (source, target) in enumerate(
+            [
+                (seq_hbm, seq_ref),
+                (sparse_hbm, sparse_ref),
+                (fwd_hbm, fwd_ref),
+                (table_hbm, table_ref),
+                (owner_hbm, owner_ref),
+                (mom_hbm, mom_ref),
+            ]
+        )
+    ]
+    for load in loads:
+        load.start()
+
     barrier = pltpu.get_barrier_semaphore()
 
     def greet(step, _):
@@ -82,6 +111,7 @@
 
     lax.fori_loop(1, nsite, greet, 0)
 
+    loads[0].wait()
     flat = seq_ref.shape[1]
     for c in range(pitch):
         low = c * LANES
@@ -95,25 +125,8 @@
         msg32[pl.ds(c, nsite, stride=pitch), :] = piece
     msgs[...] = msg32[...].reshape(nsite, pitch, LANES).astype(BF16)
 
-    pl.semaphore_wait(barrier, nsite - 1)
-
-    def seq_copy(slot, peer):
-        return pltpu.make_async_remote_copy(
-            src_ref=msgs.at[peer],
-            dst_ref=got.at[slot],
-            send_sem=send1.at[peer],
-            recv_sem=recv1.at[slot],
-            device_id={"site": peer},
-            device_id_type=pl.DeviceIdType.MESH,
-        )
-
-    def send_seq(step, _):
-        dst = lax.rem(me + step, nsite)
-        seq_copy(me, dst).start()
-        return 0
-
-    lax.fori_loop(1, nsite, send_seq, 0)
-    got[me] = msgs[me]
+    for load in loads[1:]:
+        load.wait()
 
     sparse = sparse_ref[...]
     pick = onehot(iota((sites_dev, sel), 0) == sparse)
@@ -147,7 +160,28 @@
             prod[ci, low : low + ROWS, sel:] = ar * bi + ai * br
         return 0
 
-    lax.fori_loop(0, kall // ROWS, forward_part, 0)
+    lax.fori_loop(0, EARLY, forward_part, 0)
+    pl.semaphore_wait(barrier, nsite - 1)
+
+    def seq_copy(slot, peer):
+        return pltpu.make_async_remote_copy(
+            src_ref=msgs.at[peer],
+            dst_ref=got.at[slot],
+            send_sem=send1.at[peer],
+            recv_sem=recv1.at[slot],
+            device_id={"site": peer},
+            device_id_type=pl.DeviceIdType.MESH,
+        )
+
+    def send_seq(step, _):
+        dst = lax.rem(me + step, nsite)
+        seq_copy(me, dst).start()
+        return 0
+
+    lax.fori_loop(1, nsite, send_seq, 0)
+    got[me] = msgs[me]
+
+    lax.fori_loop(EARLY, kall // ROWS, forward_part, 0)
 
     spatial = lax.rem(me, per_time) * sites_dev + column(sparse)
     xs, ys, zs = spatial & (LS - 1), (spatial >> 6) & (LS - 1), (spatial >> 12) & (LS - 1)
@@ -166,16 +200,15 @@
     rank = jnp.sum(jnp.where(earlier, 1.0, 0.0), axis=0, keepdims=True).astype(I32)
     key = owner * slots + rank
 
-    def wait_seq(step, _):
-        src = lax.rem(me + nsite - step, nsite)
-        seq_copy(src, src).wait_recv()
-        return 0
-
-    lax.fori_loop(1, nsite, wait_seq, 0)
-
     per_row = LANES // slots
 
-    def select(o, total):
+    def select(step, total):
+        o = lax.rem(me + nsite - step, nsite)
+
+        @pl.when(step > 0)
+        def _():
+            seq_copy(o, o).wait_recv()
+
         rows = got[o].astype(F32)
         pieces = []
         group = iota((8, LANES), 1) // slots
@@ -193,22 +226,52 @@
     ts[0:half, 0:sel] = ssel[:half]
     ts[0:half, sel:] = ssel[half:]
 
+    core = lax.rem(me, 2)
+    partner = me + 1 - 2 * core
+    chip = me // 2
+    nchips = nsite // 2
+
+    def pair_copy(peer):
+        return pltpu.make_async_remote_copy(
+            src_ref=halves.at[peer],
+            dst_ref=others.at[peer],
+            send_sem=send3.at[peer],
+            recv_sem=recv3.at[peer],
+            device_id={"site": partner},
+            device_id_type=pl.DeviceIdType.MESH,
+        )
+
     def part_copy(slot, peer):
         return pltpu.make_async_remote_copy(
             src_ref=parts.at[peer],
             dst_ref=acc.at[slot],
             send_sem=send2.at[peer],
             recv_sem=recv2.at[slot],
-            device_id={"site": peer},
+            device_id={"site": 2 * peer + core},
             device_id_type=pl.DeviceIdType.MESH,
         )
 
     kpad = parts.shape[1]
     nchunks = kall // ROWS
     mine = me * kdev // ROWS
+    per_chunk = ROWS // kdev // 2
+
+    def chunk_at(step):
+        return lax.rem(mine + 1 + step, nchunks)
+
+    def forward_sums(step):
+        ci = chunk_at(step)
+        for h in range(per_chunk):
+            target = ci * per_chunk + h
+            pair_copy(target).wait_recv()
+            parts[target] = (halves[nchips + target] + others[target]).astype(BF16)
+
+            @pl.when(target != chip)
+            def _():
+                part_copy(chip, target).start()
 
     def finish(step, _):
-        ci = lax.rem(mine + 1 + step, nchunks)
+        ci = chunk_at(step)
         gs = jnp.dot(ohs[ci], ts[...], preferred_element_type=F32)
         re = jnp.zeros((ROWS, sel), F32)
         im = jnp.zeros((ROWS, sel), F32)
@@ -223,35 +286,42 @@
                 re, im = re - tr, im - tim
         block = jnp.concatenate([re, im], axis=1).astype(BF16)
         sums = jnp.dot(block, phase[...], preferred_element_type=F32)
-        for h in range(ROWS // kdev):
-            piece = sums[h * kdev : (h + 1) * kdev]
+        for h in range(per_chunk):
+            target = ci * per_chunk + h
+            low = 2 * h * kdev
+            even, odd = sums[low : low + kdev], sums[low + kdev : low + 2 * kdev]
             if kpad > kdev:
-                piece = jnp.concatenate([piece, jnp.zeros((kpad - kdev, LANES), F32)], axis=0)
-            dst = ci * (ROWS // kdev) + h
-            parts[dst] = piece.astype(BF16)
-
-            @pl.when(dst != me)
-            def _():
-                part_copy(me, dst).start()
+                blank = jnp.zeros((kpad - kdev, LANES), F32)
+                even = jnp.concatenate([even, blank], axis=0)
+                odd = jnp.concatenate([odd, blank], axis=0)
+            halves[target] = jnp.where(core == 0, odd, even)
+            halves[nchips + target] = jnp.where(core == 0, even, odd)
+            pair_copy(target).start()
+
+        @pl.when(step >= LAG)
+        def _():
+            forward_sums(step - LAG)
 
         return 0
 
     lax.fori_loop(0, nchunks, finish, 0)
-    acc[me] = parts[me]
+    for step in range(nchunks - LAG, nchunks):
+        forward_sums(step)
+    acc[chip] = parts[chip]
 
     def wait_part(step, _):
-        src = lax.rem(me + nsite - step, nsite)
+        src = lax.rem(chip + nchips - step, nchips)
         part_copy(src, src).wait_recv()
         return 0
 
-    lax.fori_loop(1, nsite, wait_part, 0)
+    lax.fori_loop(1, nchips, wait_part, 0)
 
     scale = 1.0 / math.sqrt(sel * nsite / TIMES)
     firsts, seconds = [], []
     for t in range(TIMES):
         total = jnp.zeros((kpad, LANES), F32)
-        for g in range(per_time):
-            total = total + acc[t * per_time + g].astype(F32)
+        for g in range(per_time // 2):
+            total = total + acc[t * (per_time // 2) + g].astype(F32)
         total = total[:kdev] * scale
         firsts.append(total[:, :moms])
         seconds.append(total[:, moms:])
@@ -260,10 +330,20 @@
     def drain(step, _):
         dst = lax.rem(me + step, nsite)
         seq_copy(me, dst).wait_send()
-        part_copy(me, dst).wait_send()
         return 0
 
     lax.fori_loop(1, nsite, drain, 0)
+
+    def drain_pairs(target, _):
+        pair_copy(target).wait_send()
+
+        @pl.when(target != chip)
+        def _():
+            part_copy(chip, target).wait_send()
+
+        return 0
+
+    lax.fori_loop(0, nchips, drain_pairs, 0)
 
 
 def shards(forward, seqprop, sparse, owners, contraction, momenta):
@@ -281,9 +361,16 @@
     return pl.pallas_call(
         functools.partial(kernel, nsite),
         out_shape=jax.ShapeDtypeStruct((kdev, 2 * TIMES * moms), F32),
-        in_specs=[vmem] * 6,
+        in_specs=[pl.BlockSpec(memory_space=pltpu.HBM)] * 6,
         out_specs=vmem,
         scratch_shapes=[
+            pltpu.VMEM(forward.shape, BF16),
+            pltpu.VMEM(seqprop.shape, BF16),
+            pltpu.VMEM((1, kept), I32),
+            pltpu.VMEM((1, kept), I32),
+            pltpu.VMEM((TERMS, 3, kall), I32),
+            pltpu.VMEM((3, moms), I32),
+            pltpu.SemaphoreType.DMA((6,)),
             pltpu.VMEM((nsite * pitch, LANES), F32),
             pltpu.VMEM((nsite, pitch, LANES), BF16),
             pltpu.VMEM((nsite, pitch, LANES), BF16),
@@ -296,15 +383,19 @@
             pltpu.VMEM((nchunks, TERMS * ROWS, DEPTH), BF16),
             pltpu.VMEM((2 * TERMS * ROWS, 2 * kept), F32),
             pltpu.VMEM((nchunks, TERMS * ROWS, 2 * kept), F32),
-            pltpu.VMEM((nsite, kpad, LANES), BF16),
-            pltpu.VMEM((nsite, kpad, LANES), BF16),
+            pltpu.VMEM((nsite, kpad, LANES), F32),
+            pltpu.VMEM((nsite // 2, kpad, LANES), F32),
+            pltpu.VMEM((nsite // 2, kpad, LANES), BF16),
+            pltpu.VMEM((nsite // 2, kpad, LANES), BF16),
             pltpu.SemaphoreType.DMA((nsite,)),
             pltpu.SemaphoreType.DMA((nsite,)),
-            pltpu.SemaphoreType.DMA((nsite,)),
-            pltpu.SemaphoreType.DMA((nsite,)),
+            pltpu.SemaphoreType.DMA((nsite // 2,)),
+            pltpu.SemaphoreType.DMA((nsite // 2,)),
+            pltpu.SemaphoreType.DMA((nsite // 2,)),
+            pltpu.SemaphoreType.DMA((nsite // 2,)),
         ],
         compiler_params=pltpu.CompilerParams(
-            collective_id=0, has_side_effects=True, vmem_limit_bytes=48 * 1024 * 1024
+            collective_id=0, has_side_effects=True, vmem_limit_bytes=63 * 1024 * 1024
         ),
     )(
         forward,

time: 28.1 us -> 23.3 us (0.83)
  the two profiles are of different devices: /device:TPU:1 before, /device:TPU:0 now
where the time goes in v2:
time: 23.3 us; the launch traced here: 23.1 us
  Pallas kernels  21.6 us (93%)
  local copies, waits for them, and re-layouts  1.57 us (7%)
    pallas_call x1, Pallas kernels, shards(): pl.pallas_call(functools.partial(kernel, nsite), out_shape=jax.ShapeDtype...  21.6 us
    unnamed x1, local copies, waits for them, and re-layouts  1.57 us

profile of v2, /device:TPU:0, one launch (start us, length us, event | category | flops | bytes accessed | tf_op | source)
XLA Modules:
  0.0 23.1 jit_solution(15585201746554657780)
XLA Ops:
  0.0 21.6 %shard_map.64 = f32[64,512]{1,0:T(8,128)} custom-call(bf16[288,2048]{1,0:T(8,128)(2,1)} %fwd_hbm.1, bf16[16,4608]{1,0:T(8,128)(2,1)} %seq_hbm.1, s32[1,128]{1,0:T(1,128)} %bitcast.6, s32[1,128]{1,0:T(1,128)} %bitcast.7, s32[6,3,1024]{2,1,0:T(4,128)} %bitcast.4, s32[3,64]{1,0:T(4,128)} %bitcast.5), custom_call_target="tpu_custom_call" | custom-call | tf_op jit(solution)/shard_map/pallas_call | solution.py:361
  21.6 1.6 %copy.8 = f32[64,512]{1,0:T(8,128)} copy(f32[64,512]{1,0:T(8,128)} %shard_map.64) | data formatting | bytes 262144

commit v3 on v2

--- a/solution.py
+++ b/solution.py
@@ -221,7 +221,7 @@
         match = onehot(o * slots + iota((LANES, sel), 0) % slots == key)
         return total + jnp.dot(spread, match, preferred_element_type=F32)
 
-    ssel = lax.fori_loop(0, nsite, select, jnp.zeros((comps, sel), F32)).astype(BF16)
+    ssel = lax.fori_loop(0, nsite, select, jnp.zeros((comps, sel), F32), unroll=4).astype(BF16)
     ts[...] = jnp.zeros_like(ts)
     ts[0:half, 0:sel] = ssel[:half]
     ts[0:half, sel:] = ssel[half:]

time: 23.3 us -> 22.9 us (0.983)
  Pallas kernels: 21.6 us -> 21.2 us
    pallas_call x1, Pallas kernels: 21.6 us -> 21.2 us  [shards(): pl.pallas_call(functools.partial(kernel, nsite), out_shape=jax.ShapeDtype...]
where the time goes in v3:
time: 22.9 us; the launch traced here: 22.8 us
  Pallas kernels  21.2 us (93%)
  local copies, waits for them, and re-layouts  1.57 us (7%)
    pallas_call x1, Pallas kernels, shards(): pl.pallas_call(functools.partial(kernel, nsite), out_shape=jax.ShapeDtype...  21.2 us
    unnamed x1, local copies, waits for them, and re-layouts  1.57 us

profile of v3, /device:TPU:0, one launch (start us, length us, event | category | flops | bytes accessed | tf_op | source)
XLA Modules:
  0.0 22.8 jit_solution(12381817503540225905)
XLA Ops:
  0.0 21.2 %shard_map.64 = f32[64,512]{1,0:T(8,128)} custom-call(bf16[288,2048]{1,0:T(8,128)(2,1)} %fwd_hbm.1, bf16[16,4608]{1,0:T(8,128)(2,1)} %seq_hbm.1, s32[1,128]{1,0:T(1,128)} %bitcast.6, s32[1,128]{1,0:T(1,128)} %bitcast.7, s32[6,3,1024]{2,1,0:T(4,128)} %bitcast.4, s32[3,64]{1,0:T(4,128)} %bitcast.5), custom_call_target="tpu_custom_call" | custom-call | tf_op jit(solution)/shard_map/pallas_call | solution.py:361
  21.2 1.6 %copy.8 = f32[64,512]{1,0:T(8,128)} copy(f32[64,512]{1,0:T(8,128)} %shard_map.64) | data formatting | bytes 262144
